TPU v7x, 32 devices: a whole 2x2x4 slice. The times are simulated.
32 devices in a mesh: grp: 2 (over y), sub: 4 (over z), ex: 4 (over x, core).
Axes of the slice: x: 2, y: 2, z: 4, core: 2. Of those that a mesh axis runs over, the one named last changes fastest.
Arguments:
- design: bfloat16 [2560, 28672], P('sub', 'ex'), as said below
- margins: float32 [2560, 512], P('sub'), may hold values from -6 to 6
- test_ids: int32 [512], P('grp'), parts along dimension 0, may hold values from 0 to 511
- l1_penalty: float32 [512], P('grp'), parts along dimension 0, may hold values from 0.05 to 1
- l2_penalty: float32 [512], P('grp'), parts along dimension 0, may hold values from 0.1 to 3
Outputs:
- coefficients: float32 [4, 7168, 512], P('ex', 'sub', 'grp'), parts along dimension 2
There are 2 independent parts, one for each index of `grp`. A program takes and returns all parts, laid end to end along the dimension named above; an argument that names none is the same for every part. Nothing has to cross between parts.
Inputs may be any that keep to these rules, and one draw needn't show every extreme that they name: `design`: each entry is (m - a) / sqrt(a (1 - a)) / sqrt(2560) for a 0/1 inclusion m and a fixed inclusion rate a of the draw.
All inputs are finite; a program needn't handle non-finite values.
Results may differ from a plain program's by a relative error of at most 0.007.
Values may be sent and summed in bfloat16 or wider, within the bound.
A program may use at most 64 MiB of HBM per device.

v0:
```python
import jax
import jax.numpy as jnp
from jax import lax
from jax.sharding import PartitionSpec as P

step_size = 0.3


def shrink(values, l1_penalty, l2_penalty):
    limit = step_size * l1_penalty
    kept = jnp.maximum(values - limit, 0.0) - jnp.maximum(-values - limit, 0.0)
    return kept / (1.0 + step_size * l2_penalty)


def local(design, margins, test_ids, l1_penalty, l2_penalty):
    target = jnp.take(margins, test_ids, axis=1)
    start = (-target).astype(jnp.bfloat16)

    def gradient_rows(resid_half):
        return lax.psum_scatter(
            lax.dot_general(
                design, resid_half, (((0,), (0,)), ((), ())), preferred_element_type=jnp.float32
            ),
            "sub",
            scatter_dimension=0,
            tiled=True,
        )

    coef_one = shrink(-step_size * gradient_rows(start), l1_penalty, l2_penalty)
    predicted = jnp.dot(
        design,
        lax.all_gather(coef_one.astype(jnp.bfloat16), "sub", axis=0, tiled=True),
        preferred_element_type=jnp.float32,
    )
    summed = lax.psum(predicted, "ex")
    resid_half = (summed - target).astype(jnp.bfloat16)
    coef_two = shrink(coef_one - step_size * gradient_rows(resid_half), l1_penalty, l2_penalty)
    return coef_two[None]


def solution(mesh):
    in_specs = (P("sub", "ex"), P("sub", None), P("grp"), P("grp"), P("grp"))
    out_specs = P("ex", "sub", "grp")
    return jax.shard_map(local, mesh=mesh, in_specs=in_specs, out_specs=out_specs, check_vma=False)
```

profile of v0, /device:TPU:0, one launch (start us, length us, event | category | flops | bytes accessed | tf_op | source)
XLA Modules:
  0.0 416.4 jit_solution(10726807878146989712)
XLA Ops:
  6.5 0.0 reduce-scatter.3.cloned.1.call-start
  6.5 0.7 compare_and_fusion
  7.2 0.7 compare_select_fusion
  7.9 1.7 copy.6
  9.6 1.1 gather_fusion
  10.7 8.8 %convolution_bitcast_fusion.1 = f32[7168,256]{0,1:T(8,128)} fusion(bf16[640,7168]{1,0:T(8,128)(2,1)} %param.5, f32[256,640]{1,0:T(8,128)S(1)} %gather_fusion, pred[256]{0:T(512)(128)(4,1)S(1)} %compare_and_fusion), kind=kOutput, calls=%fused_computation.2 | convolution fusion | flops 2349301760 | bytes 17170688 | tf_op jit(solution)/shard_map/dot_general | solution.py:21
  19.6 0.0 copy-start
  19.6 0.0 copy-start.1
  19.6 0.0 reduce-scatter.3.cloned.1.call-update
  19.6 0.0 all-gather.2.cloned.1.call-start
  19.7 0.6 copy-done
  20.3 0.0 copy-done.1
  20.3 129.9 %reduce-scatter.3.cloned.1.call-done = f32[1792,256]{0,1:T(8,128)} async-done(((f32[7168,256]{0,1:T(8,128)}), f32[1792,256]{0,1:T(8,128)}) %reduce-scatter.3.cloned.1.call-update) | async-done | bytes 1835024 | tf_op jit(solution)/shard_map/reduce_scatter | solution.py:20
  150.2 3.1 fusion.10
  153.3 0.0 all-gather.2.cloned.1.call-update
  153.3 0.0 all-reduce.2.cloned.1.call-start
  153.3 72.7 %all-gather.2.cloned.1.call-done = bf16[7168,256]{0,1:T(8,128)(2,1)} async-done(((bf16[1792,256]{0,1:T(8,128)(2,1)}), bf16[7168,256]{0,1:T(8,128)(2,1)}) %all-gather.2.cloned.1.call-update) | async-done | bytes 3670032 | tf_op jit(solution)/shard_map/all_gather | solution.py:32
  226.1 8.6 %convolution_bitcast_fusion.2 = f32[640,256]{0,1:T(8,128)} fusion(bf16[7168,256]{0,1:T(8,128)(2,1)} %all-gather.2.cloned.1.call-done, bf16[640,7168]{1,0:T(8,128)(2,1)} %param.5), kind=kOutput, calls=%fused_computation.5 | convolution fusion | flops 2348810240 | bytes 13500416 | tf_op jit(solution)/shard_map/dot_general | solution.py:30
  234.7 0.0 all-reduce.2.cloned.1.call-update
  234.7 0.0 reduce-scatter.5.cloned.1.call-start
  234.8 32.5 %all-reduce.2.cloned.1.call-done = f32[640,256]{0,1:T(8,128)} async-done(((f32[640,256]{0,1:T(8,128)}), f32[640,256]{0,1:T(8,128)}) %all-reduce.2.cloned.1.call-update) | async-done | bytes 655376 | tf_op jit(solution)/shard_map/psum | solution.py:35
  267.2 9.9 %convolution_bitcast_fusion = f32[7168,256]{0,1:T(8,128)} fusion(bf16[640,7168]{1,0:T(8,128)(2,1)} %param.5, f32[640,256]{0,1:T(8,128)} %all-reduce.2.cloned.1.call-done, f32[256,640]{1,0:T(8,128)S(1)} %gather_fusion, pred[256]{0:T(512)(128)(4,1)S(1)} %compare_and_fusion), kind=kOutput, calls=%fused_computation.1 | convolution fusion | flops 2349301760 | bytes 17826048 | tf_op jit(solution)/shard_map/dot_general | solution.py:21
  277.1 0.0 reduce-scatter.5.cloned.1.call-update
  277.1 127.9 %reduce-scatter.5.cloned.1.call-done = f32[1792,256]{0,1:T(8,128)} async-done(((f32[7168,256]{0,1:T(8,128)}), f32[1792,256]{0,1:T(8,128)}) %reduce-scatter.5.cloned.1.call-update) | async-done | bytes 1835024 | tf_op jit(solution)/shard_map/reduce_scatter | solution.py:20
  405.0 3.2 divide_bitcast_fusion
  408.2 1.7 copy.7
  (2 shorter events, 0.0 us)
Async XLA Ops:
  6.5 143.7 %reduce-scatter.3.cloned.1.call-start = ((), (), s32[]{:S(2)}) async-start(), calls=%async_computation.2 | async-start | bytes 9175040 | tf_op jit(solution)/shard_map/reduce_scatter | solution.py:20
  19.6 0.7 copy-start
  19.6 0.7 copy-start.1
  19.6 206.5 %all-gather.2.cloned.1.call-start = ((), (), s32[]{:S(2)}) async-start(), calls=%async_computation.3 | async-start | bytes 4587520 | tf_op jit(solution)/shard_map/all_gather | solution.py:32
  153.3 113.9 %all-reduce.2.cloned.1.call-start = ((), (), s32[]{:S(2)}) async-start(), calls=%async_computation.4 | async-start | bytes 1310720 | tf_op jit(solution)/shard_map/psum | solution.py:35
  234.7 170.3 %reduce-scatter.5.cloned.1.call-start = ((), (), s32[]{:S(2)}) async-start(), calls=%async_computation.5 | async-start | bytes 9175040 | tf_op jit(solution)/shard_map/reduce_scatter | solution.py:20
Sparse Core Ops, SparseCore 0:
  19.7 130.4 reduce-scatter.2
  153.4 72.6 all-gather.1
  234.8 32.3 all-reduce.1
  277.2 127.7 reduce-scatter.4
where the time goes:
time: 417 us; the launch traced here: 416 us
  waiting for transfers between devices  363 us (87%)
  matrix products  27.3 us (7%)
  between operations  13.1 us (3%)
  other arithmetic  7.61 us (2%)
  local copies, waits for them, and re-layouts  5.11 us (1%)
    reduce_scatter x2, waiting for transfers between devices, gradient_rows(): lax.psum_scatter(lax.dot_general(design, resid_half, (((0,), (0,)), ((),...  258 us
    all_gather x1, waiting for transfers between devices, local(): lax.all_gather(coef_one.astype(jnp.bfloat16), 'sub', axis=0, tiled=True)  72.7 us
    psum x1, waiting for transfers between devices, local(): summed = lax.psum(predicted, 'ex')  32.5 us
    dot_general x2, matrix products, gradient_rows(): lax.dot_general(design, resid_half, (((0,), (0,)), ((), ())), preferred_e...  18.7 us
    dot_general x1, matrix products, local(): jnp.dot(design, lax.all_gather(coef_one.astype(jnp.bfloat16), 'sub', axis...  8.6 us
  transfers between devices with their start and end apart: 4, of which 4 were waited for; matrix products, arithmetic and copies ran while one was open for 0% of the time, Pallas kernels for 0%

commit v1 on v0

v1 whole, which is shorter than its diff:
```python
import functools

import jax
import jax.numpy as jnp
from jax import lax
from jax.experimental import pallas as pl
from jax.experimental.pallas import tpu as pltpu
from jax.sharding import PartitionSpec as P

step_size = 0.3
MESH = pl.DeviceIdType.MESH
CHUNK = 256
AHEAD = 3
F32 = jnp.float32
BF16 = jnp.bfloat16


def shrink(values, l1_penalty, l2_penalty):
    limit = step_size * l1_penalty
    kept = jnp.maximum(values - limit, 0.0) - jnp.maximum(-values - limit, 0.0)
    return kept / (1.0 + step_size * l2_penalty)


def gathered(design, margins, test_ids, l1_penalty, l2_penalty):
    target = jnp.take(margins, test_ids, axis=1)
    start = (-target).astype(BF16)

    def gradient_rows(resid_half):
        return lax.psum_scatter(
            lax.dot_general(design, resid_half, (((0,), (0,)), ((), ())), preferred_element_type=F32),
            "sub",
            scatter_dimension=0,
            tiled=True,
        )

    coef_one = shrink(-step_size * gradient_rows(start), l1_penalty, l2_penalty)
    predicted = jnp.dot(
        design,
        lax.all_gather(coef_one.astype(BF16), "sub", axis=0, tiled=True),
        preferred_element_type=F32,
    )
    summed = lax.psum(predicted, "ex")
    resid_half = (summed - target).astype(BF16)
    coef_two = shrink(coef_one - step_size * gradient_rows(resid_half), l1_penalty, l2_penalty)
    return coef_two[None]


def kernel(
    n_sub, chunks, design, margins, ids, l1, l2, out,
    full, start, target, pred, coef,
    send_a, recv_a, keep_b, send_b, recv_b, keep_c, send_c, recv_c, resid,
    own_sem, z_send, z_recv, y_send, y_recv, s_send, s_recv, e_send, e_recv, r_send, r_recv, c_send, c_recv, d_send, d_recv,
):
    g = lax.axis_index("grp")
    s = lax.axis_index("sub")
    e = lax.axis_index("ex")
    core = lax.rem(e, 2)
    col = lax.div(e, 2)
    rows = design.shape[0]
    half = rows // 2
    tests = out.shape[0]
    width = chunks * CHUNK
    part = tests // 4
    own = part // n_sub

    def to_sub(k):
        return {"sub": lax.rem(s + k, n_sub)}

    def to_ex(j):
        return {"ex": lax.rem(e + j, 4)}

    to_core = {"ex": col * 2 + 1 - core}
    to_col = {"ex": (1 - col) * 2 + core}
    to_grp = {"grp": 1 - g}

    def remote(src, dst, send, recv, device):
        return pltpu.make_async_remote_copy(
            src_ref=src, dst_ref=dst, send_sem=send, recv_sem=recv, device_id=device, device_id_type=MESH
        )

    barrier = pltpu.get_barrier_semaphore()
    for device in [to_sub(k) for k in range(1, n_sub)] + [to_ex(j) for j in range(1, 4)] + [to_grp]:
        pl.semaphore_signal(barrier, inc=1, device_id=device, device_id_type=MESH)
    pl.semaphore_wait(barrier, n_sub + 3)

    def own_copy(c):
        return pltpu.make_async_copy(
            design.at[:, pl.ds(pl.multiple_of(s * width + c * CHUNK, CHUNK), CHUNK)],
            full.at[c, s],
            own_sem.at[c],
        )

    def z_copy(c, k):
        peer = lax.rem(s + k, n_sub)
        return remote(
            design.at[pl.ds(pl.multiple_of(g * half, 16), half), pl.ds(pl.multiple_of(peer * width + c * CHUNK, CHUNK), CHUNK)],
            full.at[c, s, pl.ds(pl.multiple_of(g * half, 16), half)],
            z_send.at[c, k - 1],
            z_recv.at[c, k - 1],
            {"sub": peer},
        )

    def y_copy(c, k):
        block = full.at[c, lax.rem(s + n_sub - k, n_sub), pl.ds(pl.multiple_of(g * half, 16), half)]
        return remote(block, block, y_send.at[c, k - 1], y_recv.at[c, k - 1], to_grp)

    hops = range(1, n_sub)
    hot = (lax.broadcasted_iota(jnp.int32, (tests, margins.shape[1]), 1) == ids[...]).astype(F32)
    own_target = lax.dot_general(
        hot, margins[...], (((1,), (1,)), ((), ())), precision=lax.Precision.HIGHEST, preferred_element_type=F32
    )
    target[...] = own_target
    start[s] = (-own_target).astype(BF16)

    quarter = pl.ds(pl.multiple_of(e * part, 16), part)

    def s_copy(k):
        block = start.at[s, quarter]
        return remote(block, block, s_send.at[k - 1], s_recv.at[k - 1], to_sub(k))

    def e_copy(j, k):
        block = start.at[lax.rem(s + k, n_sub), quarter]
        return remote(block, block, e_send.at[j - 1, k - 1], e_recv.at[j - 1, k - 1], to_ex(j))

    for k in hops:
        s_copy(k).start()
    for c in range(min(AHEAD, chunks)):
        for k in hops:
            z_copy(c, k).start()
    for c in range(chunks):
        own_copy(c).start()
    for k in hops:
        s_copy(k).wait()
    for j in range(1, 4):
        for k in hops:
            e_copy(j, k).start()

    first = jnp.where(e == 0, 1.0, 0.0).astype(F32)
    for i in range(n_sub):
        pred[i] = jnp.zeros(pred.shape[1:], F32)
    pred[s] = target[...] * (-first)
    limit = step_size * l1[...]
    scale = 1.0 / (1.0 + step_size * l2[...])

    def prox(values):
        return (jnp.maximum(values - limit, 0.0) - jnp.maximum(-values - limit, 0.0)) * scale

    for j in range(1, 4):
        for k in hops:
            e_copy(j, k).wait()

    def pass_on(c):
        for k in hops:
            z_copy(c, k).wait()
            y_copy(c, k).start()

    def work(c):
        own_copy(c).wait()
        for k in hops:
            y_copy(c, k).wait()
        grad = jnp.dot(start[0], full[c, 0], preferred_element_type=F32)
        for i in range(1, n_sub):
            grad += jnp.dot(start[i], full[c, i], preferred_element_type=F32)
        one = prox(-step_size * grad)
        coef[c] = one
        one_half = one.astype(BF16)
        for i in range(n_sub):
            pred[i] += lax.dot_general(one_half, full[c, i], (((1,), (1,)), ((), ())), preferred_element_type=F32)

    pass_on(0)

    def step(c, carry):
        @pl.when(c + AHEAD - 1 < chunks)
        def _():
            for k in hops:
                z_copy(c + AHEAD - 1, k).start()

        pass_on(c)
        work(c - 1)
        return carry

    lax.fori_loop(1, chunks, step, 0)
    work(chunks - 1)

    def rows_of(first_row, count):
        return pl.ds(pl.multiple_of(first_row, 16), count)

    def a_copy(i):
        return remote(send_a.at[i], recv_a.at[i], r_send.at[0, i], r_recv.at[0, i], to_core)

    def b_copy(i):
        return remote(send_b.at[i], recv_b.at[i], r_send.at[1, i], r_recv.at[1, i], to_col)

    def c_copy(i, k):
        peer = lax.rem(s + k, n_sub)
        return remote(
            send_c.at[i, rows_of(peer * own, own)], recv_c.at[i, k - 1], c_send.at[i, k - 1], c_recv.at[i, k - 1], to_sub(k)
        )

    base = core * (2 * part) + col * part

    def d_copy(i, k):
        block = resid.at[i, rows_of(base + s * own, own)]
        return remote(block, block, d_send.at[i, k - 1], d_recv.at[i, k - 1], to_sub(k))

    def e2_copy(i):
        block = resid.at[i, rows_of(base, part)]
        return remote(block, block, r_send.at[2, i], r_recv.at[2, i], to_col)

    def f_copy(i):
        block = resid.at[i, rows_of(core * (2 * part), 2 * part)]
        return remote(block, block, r_send.at[3, i], r_recv.at[3, i], to_core)

    def stage_a(i):
        send_a[i] = pred[i, rows_of((1 - core) * (2 * part), 2 * part)].astype(BF16)
        a_copy(i).start()

    def stage_b(i):
        a_copy(i).wait()
        there = rows_of((1 - col) * part, part)
        here = rows_of(col * part, part)
        send_b[i] = (pred[i, rows_of(core * (2 * part) + (1 - col) * part, part)] + recv_a[i, there].astype(F32)).astype(BF16)
        b_copy(i).start()
        keep_b[i] = pred[i, rows_of(base, part)] + recv_a[i, here].astype(F32)

    def stage_c(i):
        b_copy(i).wait()
        total = keep_b[i] + recv_b[i].astype(F32)
        send_c[i] = total.astype(BF16)
        for k in hops:
            c_copy(i, k).start()
        keep_c[i] = total

    def stage_d(i):
        total = keep_c[i, rows_of(s * own, own)]
        for k in hops:
            c_copy(i, k).wait()
            total += recv_c[i, k - 1].astype(F32)
        resid[i, rows_of(base + s * own, own)] = total.astype(BF16)
        for k in hops:
            d_copy(i, k).start()

    def stage_e(i):
        for k in hops:
            d_copy(i, k).wait()
        e2_copy(i).start()

    def stage_f(i):
        e2_copy(i).wait()
        f_copy(i).start()

    stages = [stage_a, stage_b, stage_c, stage_d, stage_e, stage_f]
    for t in range(n_sub + len(stages) - 1):
        for number in reversed(range(len(stages))):
            if 0 <= t - number < n_sub:
                stages[number](t - number)
    for i in range(n_sub):
        f_copy(i).wait()

    def finish(c, carry):
        grad = jnp.dot(resid[0], full[c, 0], preferred_element_type=F32)
        for i in range(1, n_sub):
            grad += jnp.dot(resid[i], full[c, i], preferred_element_type=F32)
        out[:, pl.ds(pl.multiple_of(c * CHUNK, CHUNK), CHUNK)] = prox(coef[c] - step_size * grad)
        return carry

    lax.fori_loop(0, chunks, finish, 0)


def transposed(n_sub, design, margins, test_ids, l1_penalty, l2_penalty):
    rows = design.shape[0]
    width = design.shape[1] // n_sub
    chunks = width // CHUNK
    tests = test_ids.shape[0]
    part = tests // 4
    own = part // n_sub
    vmem = pl.BlockSpec(memory_space=pltpu.VMEM)
    dma = pltpu.SemaphoreType.DMA
    coef_two = pl.pallas_call(
        functools.partial(kernel, n_sub, chunks),
        out_shape=jax.ShapeDtypeStruct((tests, width), F32),
        in_specs=[pl.BlockSpec(memory_space=pl.ANY)] + [vmem] * 4,
        out_specs=vmem,
        scratch_shapes=[
            pltpu.VMEM((chunks, n_sub, rows, CHUNK), BF16),
            pltpu.VMEM((n_sub, tests, rows), BF16),
            pltpu.VMEM((tests, rows), F32),
            pltpu.VMEM((n_sub, tests, rows), F32),
            pltpu.VMEM((chunks, tests, CHUNK), F32),
            pltpu.VMEM((n_sub, 2 * part, rows), BF16),
            pltpu.VMEM((n_sub, 2 * part, rows), BF16),
            pltpu.VMEM((n_sub, part, rows), F32),
            pltpu.VMEM((n_sub, part, rows), BF16),
            pltpu.VMEM((n_sub, part, rows), BF16),
            pltpu.VMEM((n_sub, part, rows), F32),
            pltpu.VMEM((n_sub, part, rows), BF16),
            pltpu.VMEM((n_sub, n_sub - 1, own, rows), BF16),
            pltpu.VMEM((n_sub, tests, rows), BF16),
            dma((chunks,)),
            dma((chunks, n_sub - 1)),
            dma((chunks, n_sub - 1)),
            dma((chunks, n_sub - 1)),
            dma((chunks, n_sub - 1)),
            dma((n_sub - 1,)),
            dma((n_sub - 1,)),
            dma((3, n_sub - 1)),
            dma((3, n_sub - 1)),
            dma((4, n_sub)),
            dma((4, n_sub)),
            dma((n_sub, n_sub - 1)),
            dma((n_sub, n_sub - 1)),
            dma((n_sub, n_sub - 1)),
            dma((n_sub, n_sub - 1)),
        ],
        compiler_params=pltpu.CompilerParams(
            collective_id=0, has_side_effects=True, vmem_limit_bytes=48 * 1024 * 1024
        ),
    )(design, margins, test_ids[:, None], l1_penalty[:, None], l2_penalty[:, None])
    return coef_two.T[None]


def solution(mesh):
    n_sub = mesh.shape["sub"]

    def local(design, margins, test_ids, l1_penalty, l2_penalty):
        width = design.shape[1] // n_sub
        fits = (
            mesh.shape["grp"] == 2
            and mesh.shape["ex"] == 4
            and n_sub > 1
            and width % CHUNK == 0
            and design.shape[0] % 128 == 0
            and test_ids.shape[0] % (64 * n_sub) == 0
        )
        if fits:
            return transposed(n_sub, design, margins, test_ids, l1_penalty, l2_penalty)
        return gathered(design, margins, test_ids, l1_penalty, l2_penalty)

    in_specs = (P("sub", "ex"), P("sub", None), P("grp"), P("grp"), P("grp"))
    out_specs = P("ex", "sub", "grp")
    return jax.shard_map(local, mesh=mesh, in_specs=in_specs, out_specs=out_specs, check_vma=False)
```

time: 417 us -> 178 us (0.43)
  waiting for transfers between devices: 363 us -> 0 us
  Pallas kernels: 0 us -> 172 us
  matrix products: 27.3 us -> 0 us
  between operations: 13.1 us -> 0.04 us
  other arithmetic: 7.61 us -> 0 us
    reduce_scatter x2 -> x0, waiting for transfers between devices: 258 us -> none  [gradient_rows(): lax.psum_scatter(lax.dot_general(design, resid_half, (((0,), (0,)), ((),...]
    pallas_call x0 -> x1, Pallas kernels: none -> 172 us  [transposed(): pl.pallas_call(functools.partial(kernel, n_sub, chunks), out_shape=jax.Sh...]
    all_gather x1 -> x0, waiting for transfers between devices: 72.7 us -> none  [local(): lax.all_gather(coef_one.astype(jnp.bfloat16), 'sub', axis=0, tiled=True)]
    psum x1 -> x0, waiting for transfers between devices: 32.5 us -> none  [local(): summed = lax.psum(predicted, 'ex')]
    dot_general x3 -> x0, matrix products: 27.3 us -> none  [the longest x2 18.7 us: gradient_rows(): lax.dot_general(design, resid_half, (((0,), (0,)), ((), ())), preferred_e...]
  transfers between devices with their start and end apart: 4 -> 0, of which waited for: 4 -> 0; matrix products, arithmetic and copies ran while one was open for 0% -> 0% of each run, Pallas kernels for 0% -> 0%
where the time goes in v1:
time: 178 us; the launch traced here: 177 us
  Pallas kernels  172 us (97%)
  local copies, waits for them, and re-layouts  5.43 us (3%)
    pallas_call x1, Pallas kernels, transposed(): pl.pallas_call(functools.partial(kernel, n_sub, chunks), out_shape=jax.Sh...  172 us

profile of v1, /device:TPU:0, one launch (start us, length us, event | category | flops | bytes accessed | tf_op | source)
XLA Modules:
  0.0 177.4 jit_solution(17210580345234792187)
XLA Ops:
  0.0 0.8 copy.7.ids
  0.8 0.8 copy.8.l1
  1.6 0.8 copy.9.l2
  2.5 0.0 copy-start
  2.5 1.3 copy-done
  3.8 172.0 %shard_map.55 = f32[256,1792]{1,0:T(8,128)S(1)} custom-call(bf16[640,7168]{1,0:T(8,128)(2,1)} %design.1, f32[640,512]{1,0:T(8,128)S(1)} %copy-done, s32[256,1]{1,0:T(8,128)S(1)} %copy.7.ids, f32[256,1]{1,0:T(8,128)S(1)} %copy.8.l1, f32[256,1]{1,0:T(8,128)S(1)} %copy.9.l2), custom_call_target="tpu_custom_call" | custom-call | tf_op jit(solution)/shard_map/pallas_call | solution.py:279
  175.7 1.7 copy.10
Async XLA Ops:
  2.5 1.3 copy-start

commit v2 on v1

--- a/solution.py
+++ b/solution.py
@@ -10,7 +10,8 @@
 step_size = 0.3
 MESH = pl.DeviceIdType.MESH
 CHUNK = 256
-AHEAD = 3
+AHEAD = 2
+PIECES = 2
 F32 = jnp.float32
 BF16 = jnp.bfloat16
 
@@ -47,7 +48,7 @@
 
 def kernel(
     n_sub, chunks, design, margins, ids, l1, l2, out,
-    full, start, target, pred, coef,
+    full, start, target, pred, coef, table, table_sem,
     send_a, recv_a, keep_b, send_b, recv_b, keep_c, send_c, recv_c, resid,
     own_sem, z_send, z_recv, y_send, y_recv, s_send, s_recv, e_send, e_recv, r_send, r_recv, c_send, c_recv, d_send, d_recv,
 ):
@@ -81,6 +82,28 @@
     barrier = pltpu.get_barrier_semaphore()
     for device in [to_sub(k) for k in range(1, n_sub)] + [to_ex(j) for j in range(1, 4)] + [to_grp]:
         pl.semaphore_signal(barrier, inc=1, device_id=device, device_id_type=MESH)
+
+    fetch = pltpu.make_async_copy(margins, table, table_sem)
+    fetch.start()
+    eye = lax.broadcasted_iota(jnp.int32, (tests, tests), 0) == lax.broadcasted_iota(jnp.int32, (tests, tests), 1)
+
+    def column(row):
+        return jnp.sum(jnp.where(eye, row, 0.0), axis=1, keepdims=True)
+
+    limit = step_size * column(l1[...])
+    scale = 1.0 / (1.0 + step_size * column(l2[...]))
+    wanted = column(ids[...].astype(F32))
+    hot = (lax.broadcasted_iota(jnp.int32, (tests, margins.shape[1]), 1).astype(F32) == wanted).astype(F32)
+    fetch.wait()
+    own_target = lax.dot_general(
+        hot, table[...], (((1,), (1,)), ((), ())), precision=lax.Precision.HIGHEST, preferred_element_type=F32
+    )
+    target[...] = own_target
+    start[s] = (-own_target).astype(BF16)
+    first = jnp.where(e == 0, 1.0, 0.0).astype(F32)
+    for i in range(n_sub):
+        pred[i] = jnp.zeros(pred.shape[1:], F32)
+    pred[s] = target[...] * (-first)
     pl.semaphore_wait(barrier, n_sub + 3)
 
     def own_copy(c):
@@ -90,28 +113,31 @@
             own_sem.at[c],
         )
 
-    def z_copy(c, k):
+    piece = half // PIECES
+
+    def rows_at(h):
+        return pl.ds(pl.multiple_of(g * half + h * piece, 16), piece)
+
+    def z_copy(c, h, k):
         peer = lax.rem(s + k, n_sub)
         return remote(
-            design.at[pl.ds(pl.multiple_of(g * half, 16), half), pl.ds(pl.multiple_of(peer * width + c * CHUNK, CHUNK), CHUNK)],
-            full.at[c, s, pl.ds(pl.multiple_of(g * half, 16), half)],
-            z_send.at[c, k - 1],
-            z_recv.at[c, k - 1],
+            design.at[rows_at(h), pl.ds(pl.multiple_of(peer * width + c * CHUNK, CHUNK), CHUNK)],
+            full.at[c, s, rows_at(h)],
+            z_send.at[c, h, k - 1],
+            z_recv.at[c, h, k - 1],
             {"sub": peer},
         )
 
-    def y_copy(c, k):
-        block = full.at[c, lax.rem(s + n_sub - k, n_sub), pl.ds(pl.multiple_of(g * half, 16), half)]
-        return remote(block, block, y_send.at[c, k - 1], y_recv.at[c, k - 1], to_grp)
+    def y_copy(c, h, k):
+        block = full.at[c, lax.rem(s + n_sub - k, n_sub), rows_at(h)]
+        return remote(block, block, y_send.at[c, h, k - 1], y_recv.at[c, h, k - 1], to_grp)
+
+    def send_chunk(c):
+        for h in range(PIECES):
+            for k in hops:
+                z_copy(c, h, k).start()
 
     hops = range(1, n_sub)
-    hot = (lax.broadcasted_iota(jnp.int32, (tests, margins.shape[1]), 1) == ids[...]).astype(F32)
-    own_target = lax.dot_general(
-        hot, margins[...], (((1,), (1,)), ((), ())), precision=lax.Precision.HIGHEST, preferred_element_type=F32
-    )
-    target[...] = own_target
-    start[s] = (-own_target).astype(BF16)
-
     quarter = pl.ds(pl.multiple_of(e * part, 16), part)
 
     def s_copy(k):
@@ -125,8 +151,7 @@
     for k in hops:
         s_copy(k).start()
     for c in range(min(AHEAD, chunks)):
-        for k in hops:
-            z_copy(c, k).start()
+        send_chunk(c)
     for c in range(chunks):
         own_copy(c).start()
     for k in hops:
@@ -135,29 +160,20 @@
         for k in hops:
             e_copy(j, k).start()
 
-    first = jnp.where(e == 0, 1.0, 0.0).astype(F32)
-    for i in range(n_sub):
-        pred[i] = jnp.zeros(pred.shape[1:], F32)
-    pred[s] = target[...] * (-first)
-    limit = step_size * l1[...]
-    scale = 1.0 / (1.0 + step_size * l2[...])
-
     def prox(values):
         return (jnp.maximum(values - limit, 0.0) - jnp.maximum(-values - limit, 0.0)) * scale
 
-    for j in range(1, 4):
-        for k in hops:
-            e_copy(j, k).wait()
-
     def pass_on(c):
-        for k in hops:
-            z_copy(c, k).wait()
-            y_copy(c, k).start()
+        for h in range(PIECES):
+            for k in hops:
+                z_copy(c, h, k).wait()
+                y_copy(c, h, k).start()
 
     def work(c):
         own_copy(c).wait()
-        for k in hops:
-            y_copy(c, k).wait()
+        for h in range(PIECES):
+            for k in hops:
+                y_copy(c, h, k).wait()
         grad = jnp.dot(start[0], full[c, 0], preferred_element_type=F32)
         for i in range(1, n_sub):
             grad += jnp.dot(start[i], full[c, i], preferred_element_type=F32)
@@ -168,12 +184,14 @@
             pred[i] += lax.dot_general(one_half, full[c, i], (((1,), (1,)), ((), ())), preferred_element_type=F32)
 
     pass_on(0)
+    for j in range(1, 4):
+        for k in hops:
+            e_copy(j, k).wait()
 
     def step(c, carry):
         @pl.when(c + AHEAD - 1 < chunks)
         def _():
-            for k in hops:
-                z_copy(c + AHEAD - 1, k).start()
+            send_chunk(c + AHEAD - 1)
 
         pass_on(c)
         work(c - 1)
@@ -249,18 +267,29 @@
         e2_copy(i).wait()
         f_copy(i).start()
 
-    stages = [stage_a, stage_b, stage_c, stage_d, stage_e, stage_f]
-    for t in range(n_sub + len(stages) - 1):
-        for number in reversed(range(len(stages))):
-            if 0 <= t - number < n_sub:
-                stages[number](t - number)
-    for i in range(n_sub):
+    def second(i):
         f_copy(i).wait()
 
+        def add(c, carry):
+            coef[c] += -step_size * jnp.dot(resid[i], full[c, i], preferred_element_type=F32)
+            return carry
+
+        lax.fori_loop(0, chunks, add, 0)
+
+    offset = ((stage_a, 0.0), (stage_b, 1.0), (stage_c, 4.0), (stage_d, 7.5), (stage_e, 11.0), (stage_f, 14.0))
+    pace = (0.2, 0.3, 1.7, 2.4, 2.6, 2.6)
+    plan = [(at + pace[m] * i, m, i) for m, (stage, at) in enumerate(offset) for i in range(n_sub)]
+    for _, m, i in sorted(plan):
+        if m == len(offset) - 1 and i > 1:
+            second(i - 2)
+        offset[m][0](i)
+    for i in range(max(n_sub - 2, 0), n_sub - 1):
+        second(i)
+    last = n_sub - 1
+    f_copy(last).wait()
+
     def finish(c, carry):
-        grad = jnp.dot(resid[0], full[c, 0], preferred_element_type=F32)
-        for i in range(1, n_sub):
-            grad += jnp.dot(resid[i], full[c, i], preferred_element_type=F32)
+        grad = jnp.dot(resid[last], full[c, last], preferred_element_type=F32)
         out[:, pl.ds(pl.multiple_of(c * CHUNK, CHUNK), CHUNK)] = prox(coef[c] - step_size * grad)
         return carry
 
@@ -279,7 +308,7 @@
     coef_two = pl.pallas_call(
         functools.partial(kernel, n_sub, chunks),
         out_shape=jax.ShapeDtypeStruct((tests, width), F32),
-        in_specs=[pl.BlockSpec(memory_space=pl.ANY)] + [vmem] * 4,
+        in_specs=[pl.BlockSpec(memory_space=pl.ANY)] * 2 + [vmem] * 3,
         out_specs=vmem,
         scratch_shapes=[
             pltpu.VMEM((chunks, n_sub, rows, CHUNK), BF16),
@@ -287,6 +316,8 @@
             pltpu.VMEM((tests, rows), F32),
             pltpu.VMEM((n_sub, tests, rows), F32),
             pltpu.VMEM((chunks, tests, CHUNK), F32),
+            pltpu.VMEM(margins.shape, F32),
+            dma,
             pltpu.VMEM((n_sub, 2 * part, rows), BF16),
             pltpu.VMEM((n_sub, 2 * part, rows), BF16),
             pltpu.VMEM((n_sub, part, rows), F32),
@@ -297,10 +328,10 @@
             pltpu.VMEM((n_sub, n_sub - 1, own, rows), BF16),
             pltpu.VMEM((n_sub, tests, rows), BF16),
             dma((chunks,)),
-            dma((chunks, n_sub - 1)),
-            dma((chunks, n_sub - 1)),
-            dma((chunks, n_sub - 1)),
-            dma((chunks, n_sub - 1)),
+            dma((chunks, PIECES, n_sub - 1)),
+            dma((chunks, PIECES, n_sub - 1)),
+            dma((chunks, PIECES, n_sub - 1)),
+            dma((chunks, PIECES, n_sub - 1)),
             dma((n_sub - 1,)),
             dma((n_sub - 1,)),
             dma((3, n_sub - 1)),
@@ -315,7 +346,7 @@
         compiler_params=pltpu.CompilerParams(
             collective_id=0, has_side_effects=True, vmem_limit_bytes=48 * 1024 * 1024
         ),
-    )(design, margins, test_ids[:, None], l1_penalty[:, None], l2_penalty[:, None])
+    )(design, margins, test_ids[None], l1_penalty[None], l2_penalty[None])
     return coef_two.T[None]
 
 
@@ -329,6 +360,7 @@
             and mesh.shape["ex"] == 4
             and n_sub > 1
             and width % CHUNK == 0
+            and design.shape[0] % (32 * PIECES) == 0
             and design.shape[0] % 128 == 0
             and test_ids.shape[0] % (64 * n_sub) == 0
         )

time: 178 us -> 163 us (0.916)
  Pallas kernels: 172 us -> 157 us
    pallas_call x1, Pallas kernels: 172 us -> 157 us  [transposed(): pl.pallas_call(functools.partial(kernel, n_sub, chunks), out_shape=jax.Sh...]
    broadcast_in_dim x3 -> x0, local copies, waits for them, and re-layouts: 2.43 us -> none  [the longest x1 0.81 us: transposed(): l1_penalty[:, None]]
    unnamed x2 -> x8, local copies, waits for them, and re-layouts: 1.31 us -> 3.35 us
where the time goes in v2:
time: 163 us; the launch traced here: 162 us
  Pallas kernels  157 us (96%)
  local copies, waits for them, and re-layouts  5.04 us (3%)
    pallas_call x1, Pallas kernels, transposed(): pl.pallas_call(functools.partial(kernel, n_sub, chunks), out_shape=jax.Sh...  157 us
    unnamed x8, local copies, waits for them, and re-layouts  3.35 us

profile of v2, /device:TPU:0, one launch (start us, length us, event | category | flops | bytes accessed | tf_op | source)
XLA Modules:
  0.0 162.3 jit_solution(7010604457422474941)
XLA Ops:
  0.0 0.0 copy-start
  0.0 1.3 copy-done
  1.3 0.0 copy-start.1
  1.3 0.7 copy-done.1
  2.0 0.0 copy-start.2
  2.0 0.7 copy-done.2
  2.7 0.0 copy-start.3
  2.7 0.7 copy-done.3
  3.4 157.3 %shard_map.55 = f32[256,1792]{1,0:T(8,128)S(1)} custom-call(bf16[640,7168]{1,0:T(8,128)(2,1)} %design.1, f32[640,512]{1,0:T(8,128)S(1)} %copy-done, s32[1,256]{1,0:T(1,128)S(1)} %bitcast.7, f32[1,256]{1,0:T(1,128)S(1)} %bitcast.8, f32[1,256]{1,0:T(1,128)S(1)} %bitcast.9), custom_call_target="tpu_custom_call" | custom-call | tf_op jit(solution)/shard_map/pallas_call | solution.py:308
  160.6 1.7 %copy.6 = f32[1,1792,256]{2,1,0:T(8,128)} copy(f32[1,1792,256]{1,2,0:T(8,128)S(1)} %bitcast.6) | data formatting | bytes 3670016 | tf_op jit(solution)/shard_map/broadcast_in_dim | solution.py:350
Async XLA Ops:
  0.0 1.3 copy-start
  1.3 0.7 copy-start.1
  2.0 0.7 copy-start.2
  2.7 0.7 copy-start.3

commit v3 on v2

--- a/solution.py
+++ b/solution.py
@@ -169,7 +169,7 @@
                 z_copy(c, h, k).wait()
                 y_copy(c, h, k).start()
 
-    def work(c):
+    def work(c, done=None):
         own_copy(c).wait()
         for h in range(PIECES):
             for k in hops:
@@ -182,6 +182,8 @@
         one_half = one.astype(BF16)
         for i in range(n_sub):
             pred[i] += lax.dot_general(one_half, full[c, i], (((1,), (1,)), ((), ())), preferred_element_type=F32)
+            if done is not None:
+                done(i)
 
     pass_on(0)
     for j in range(1, 4):
@@ -198,7 +200,6 @@
         return carry
 
     lax.fori_loop(1, chunks, step, 0)
-    work(chunks - 1)
 
     def rows_of(first_row, count):
         return pl.ds(pl.multiple_of(first_row, 16), count)
@@ -232,6 +233,8 @@
     def stage_a(i):
         send_a[i] = pred[i, rows_of((1 - core) * (2 * part), 2 * part)].astype(BF16)
         a_copy(i).start()
+
+    work(chunks - 1, stage_a)
 
     def stage_b(i):
         a_copy(i).wait()
@@ -282,7 +285,8 @@
     for _, m, i in sorted(plan):
         if m == len(offset) - 1 and i > 1:
             second(i - 2)
-        offset[m][0](i)
+        if m > 0:
+            offset[m][0](i)
     for i in range(max(n_sub - 2, 0), n_sub - 1):
         second(i)
     last = n_sub - 1

time: 163 us -> 162 us (level)
  no operation moved by 1% of the time
where the time goes in v3:
time: 162 us; the launch traced here: 161 us
  Pallas kernels  156 us (96%)
  local copies, waits for them, and re-layouts  5.04 us (3%)
    pallas_call x1, Pallas kernels, transposed(): pl.pallas_call(functools.partial(kernel, n_sub, chunks), out_shape=jax.Sh...  156 us
    unnamed x8, local copies, waits for them, and re-layouts  3.35 us

profile of v3, /device:TPU:0, one launch (start us, length us, event | category | flops | bytes accessed | tf_op | source)
XLA Modules:
  0.0 161.3 jit_solution(7615019333906523706)
XLA Ops:
  0.0 0.0 copy-start
  0.0 1.3 copy-done
  1.3 0.0 copy-start.1
  1.3 0.7 copy-done.1
  2.0 0.0 copy-start.2
  2.0 0.7 copy-done.2
  2.7 0.0 copy-start.3
  2.7 0.7 copy-done.3
  3.4 156.3 %shard_map.55 = f32[256,1792]{1,0:T(8,128)S(1)} custom-call(bf16[640,7168]{1,0:T(8,128)(2,1)} %design.1, f32[640,512]{1,0:T(8,128)S(1)} %copy-done, s32[1,256]{1,0:T(1,128)S(1)} %bitcast.7, f32[1,256]{1,0:T(1,128)S(1)} %bitcast.8, f32[1,256]{1,0:T(1,128)S(1)} %bitcast.9), custom_call_target="tpu_custom_call" | custom-call | tf_op jit(solution)/shard_map/pallas_call | solution.py:312
  159.7 1.7 %copy.6 = f32[1,1792,256]{2,1,0:T(8,128)} copy(f32[1,1792,256]{1,2,0:T(8,128)S(1)} %bitcast.6) | data formatting | bytes 3670016 | tf_op jit(solution)/shard_map/broadcast_in_dim | solution.py:354
Async XLA Ops:
  0.0 1.3 copy-start
  1.3 0.7 copy-start.1
  2.0 0.7 copy-start.2
  2.7 0.7 copy-start.3
